TPU v7x, 32 devices: a whole 2x2x4 slice. The times are simulated.
32 devices in a mesh: groups: 2 (over y), seq: 16 (over z, x, core).
Axes of the slice: x: 2, y: 2, z: 4, core: 2. Of those that a mesh axis runs over, the one named last changes fastest.
Arguments:
- queries: bfloat16 [8192, 2048], P(('groups', 'seq')), parts along dimension 0, may hold values from -6 to 6
- key_inputs: bfloat16 [8192, 2048], P(('groups', 'seq')), parts along dimension 0, may hold values from -6 to 6
- values: bfloat16 [8192, 2048], P(('groups', 'seq')), parts along dimension 0, may hold values from -6 to 6
- short_taps: float32 [3, 3, 2048], replicated, may hold values from -3.6 to 3.6
- decay_rates: float32 [2, 2048], replicated, may hold values from 2.4414063e-05 to 0.05, as said below
- residues: float32 [2, 2048], replicated, may hold values from -6 to 6
- skip_gain: float32 [2048], replicated, may hold values from -6 to 6
- out_weight: bfloat16 [2048, 4096], P('seq'), may hold values from -0.125 to 0.125
- cotangent: bfloat16 [8192, 4096], P(('groups', 'seq')), parts along dimension 0, may hold values from -6 to 6
- doc_blocks: int32 [8], P('groups'), parts along dimension 0, may hold values from 1 to 16, 32 in all
Outputs:
- mixed_out: bfloat16 [8192, 4096], P(('groups', 'seq')), parts along dimension 0
- grad_queries: bfloat16 [8192, 2048], P(('groups', 'seq')), parts along dimension 0
- grad_keys: bfloat16 [8192, 2048], P(('groups', 'seq')), parts along dimension 0
- grad_values: bfloat16 [8192, 2048], P(('groups', 'seq')), parts along dimension 0
There are 2 independent parts, one for each index of `groups`. A program takes and returns all parts, laid end to end along the dimension named above; an argument that names none is the same for every part. Nothing has to cross between parts.
Inputs may be any that keep to these rules, and one draw needn't show every extreme that they name: `doc_blocks`: documents fill the batch in order: the entries sum to 32, and the longest is exactly 16 blocks. `decay_rates`: positive decay rates.
All inputs are finite; a program needn't handle non-finite values.
Results may differ from a plain program's by a relative error of at most 0.0051.
Values may be sent and summed in bfloat16 or wider, within the bound.
A program may use at most 128 MiB of HBM per device.

v0:
```python
import jax
import jax.numpy as jnp
from jax import lax
from jax.sharding import PartitionSpec as P

BLOCK = 128


exact_mode = lax.Precision.HIGHEST


def from_behind(value, axis, steps):
    count = lax.axis_size(axis)
    leading, last = (max(0, -steps), min(count, count - steps))
    return lax.ppermute(value, axis, [(source, source + steps) for source in range(leading, last)])


def combine(earlier, later):
    return (earlier[0] * later[0], later[0] * earlier[1] + later[1])


def block_marks(doc_blocks, first_block, block_count):
    doc_ends = jnp.cumsum(doc_blocks)
    starts = doc_ends - doc_blocks
    block_index = first_block + jnp.arange(block_count, dtype=jnp.int32)
    matches = (block_index[:, None] == starts[None, :]) | (block_index[:, None] >= doc_ends[-1])
    return jnp.any(matches, axis=1).astype(jnp.float32)


def block_parts(blocked, decay_rates, reset_flags):
    span = blocked.shape[-1]
    offsets = jnp.arange(span, dtype=jnp.float32)
    upper_ones = (offsets[:, None] <= offsets[None, :]).astype(jnp.float32)
    growth = jnp.exp(decay_rates[:, :, None] * offsets[None, None, :])
    shrink = jnp.exp(-decay_rates[:, :, None] * offsets[None, None, :])
    lifted = blocked[None, :, :, :] * growth[:, :, None, :]
    inside = (
        jnp.einsum("sgbp,pt->sgbt", lifted, upper_ones, precision=exact_mode)
        * shrink[:, :, None, :]
    )
    keep_rate = (1.0 - reset_flags)[None, None, :] * jnp.exp(-decay_rates * span)[:, :, None]
    cum_keep, cum_ends = lax.associative_scan(combine, (keep_rate, inside[..., -1]), axis=2)
    return (inside, cum_keep, cum_ends)


def block_finish(inside, cum_keep, cum_ends, decay_rates, filter_weight, reset_flags, incoming):
    span = inside.shape[-1]
    at_end = cum_keep * incoming[:, :, None] + cum_ends
    before = (
        jnp.concatenate([incoming[:, :, None], at_end[:, :, :-1]], axis=2)
        * (1.0 - reset_flags)[None, None, :]
    )
    offsets = jnp.arange(1, span + 1, dtype=jnp.float32)
    decay_rows = jnp.exp(-decay_rates[:, :, None] * offsets[None, None, :])
    summed_up = inside + before[..., None] * decay_rows[:, :, None, :]
    return jnp.sum(summed_up * filter_weight[:, :, None, None], axis=0)


def relay_pass(columns, decay_rates, filter_weight, doc_blocks, backward):
    device_place = lax.axis_index("seq")
    spread = lax.all_to_all(columns, "seq", split_axis=0, concat_axis=1, tiled=True)
    share_width = spread.shape[0]
    block_count = spread.shape[1] // BLOCK
    own_rates = lax.dynamic_slice_in_dim(decay_rates, device_place * share_width, share_width, 1)
    own_weights = lax.dynamic_slice_in_dim(
        filter_weight, device_place * share_width, share_width, 1
    )
    lead_shift = 1 if backward else 0
    reset_flags = block_marks(doc_blocks, lead_shift, block_count)
    blocked = spread.reshape(share_width, block_count, BLOCK)
    if backward:
        blocked = jnp.flip(blocked, axis=(1, 2))
        reset_flags = jnp.flip(reset_flags, axis=0)
    inside, cum_keep, cum_ends = block_parts(blocked, own_rates, reset_flags)
    zero_state = jnp.zeros(own_rates.shape, jnp.float32)
    result = block_finish(
        inside, cum_keep, cum_ends, own_rates, own_weights, reset_flags, zero_state
    )
    if backward:
        result = jnp.flip(result, axis=(1, 2))
    return lax.all_to_all(
        result.reshape(share_width, block_count * BLOCK),
        "seq",
        split_axis=1,
        concat_axis=0,
        tiled=True,
    )


def long_conv(columns, decay_rates, filter_weight, doc_blocks, backward):
    return relay_pass(columns, decay_rates, filter_weight, doc_blocks, backward)


def on_device(
    queries,
    key_inputs,
    values,
    short_taps,
    decay_rates,
    residues,
    skip_gain,
    out_weight,
    cotangent,
    doc_blocks,
):
    row_count = queries.shape[0]
    block_count = row_count // BLOCK
    marks_ext = block_marks(doc_blocks, lax.axis_index("seq") * block_count, block_count + 1)
    head_mask = (jnp.arange(BLOCK) == 0).astype(jnp.float32)
    begins = (marks_ext[:, None] * head_mask[None, :]).reshape(-1)[: row_count + 2]
    now_start = begins[:row_count]
    prior_start = jnp.concatenate([jnp.zeros((1,), jnp.float32), now_start[:-1]])
    keep_one = (1.0 - now_start)[:, None]
    keep_two = keep_one * (1.0 - prior_start)[:, None]
    next_one = (1.0 - begins[1 : row_count + 1])[:, None]
    next_two = next_one * (1.0 - begins[2 : row_count + 2])[:, None]
    tail_rows = jnp.stack(
        [queries[row_count - 2 :], key_inputs[row_count - 2 :], values[row_count - 2 :]]
    )
    prev_rims = from_behind(tail_rows, "seq", 1)

    def forward_short(current, rim_rows, tap_row):
        longer = jnp.concatenate([rim_rows, current], axis=0).astype(jnp.float32)
        return (
            tap_row[0] * longer[2:]
            + tap_row[1] * keep_one * longer[1:-1]
            + tap_row[2] * keep_two * longer[:-2]
        )

    q_short = forward_short(queries, prev_rims[0], short_taps[0])
    k_short = forward_short(key_inputs, prev_rims[1], short_taps[1])
    v_short = forward_short(values, prev_rims[2], short_taps[2])
    product = k_short * v_short
    filter_weight = residues * jnp.sqrt(2.0 * decay_rates)
    conv_out = (
        long_conv(product.T, decay_rates, filter_weight, doc_blocks, False).T + skip_gain * product
    )
    gated_rows = (q_short * conv_out).astype(jnp.bfloat16)
    weight_piece = lax.all_gather(out_weight, "seq", axis=0, tiled=True)
    total_out = jnp.dot(gated_rows, weight_piece, preferred_element_type=jnp.float32)
    column = lax.dot_general(
        cotangent, weight_piece, (((1,), (1,)), ((), ())), preferred_element_type=jnp.float32
    )
    total_out, grad_gated = (total_out, column)
    mixed_out = total_out.astype(jnp.bfloat16)
    grad_qs = grad_gated * conv_out
    grad_conv = grad_gated * q_short
    grad_product = (
        long_conv(grad_conv.T, decay_rates, filter_weight, doc_blocks, True).T
        + skip_gain * grad_conv
    )
    grad_ks = grad_product * v_short
    grad_vs = grad_product * k_short
    head_rows = jnp.stack([grad_qs[:2], grad_ks[:2], grad_vs[:2]])
    next_rims = from_behind(head_rows.astype(jnp.bfloat16), "seq", -1).astype(head_rows.dtype)

    def backward_short(gradient, rim_rows, tap_row):
        longer = jnp.concatenate([gradient, rim_rows], axis=0)
        summed = (
            tap_row[0] * gradient
            + tap_row[1] * next_one * longer[1 : row_count + 1]
            + tap_row[2] * next_two * longer[2:]
        )
        return summed.astype(jnp.bfloat16)

    grad_queries = backward_short(grad_qs, next_rims[0], short_taps[0])
    grad_keys = backward_short(grad_ks, next_rims[1], short_taps[1])
    grad_values = backward_short(grad_vs, next_rims[2], short_taps[2])
    return (mixed_out, grad_queries, grad_keys, grad_values)


def solution(mesh):
    return jax.shard_map(
        on_device,
        mesh=mesh,
        in_specs=(
            P(("groups", "seq"), None),
            P(("groups", "seq"), None),
            P(("groups", "seq"), None),
            P(),
            P(),
            P(),
            P(),
            P("seq", None),
            P(("groups", "seq"), None),
            P("groups"),
        ),
        out_specs=(
            P(("groups", "seq"), None),
            P(("groups", "seq"), None),
            P(("groups", "seq"), None),
            P(("groups", "seq"), None),
        ),
        check_vma=False,
    )
```

profile of v0, /device:TPU:3, one launch (start us, length us, event | category | flops | bytes accessed | tf_op | source)
XLA Modules:
  0.0 409.5 jit_solution(16186817507365080882)
XLA Ops:
  9.6 3.7 collective-permute-start
  20.0 3.1 multiply_bitcast_fusion.1
  24.7 5.3 %all-to-all-start = ((f32[16,128,256]{1,2,0:T(8,128)}), f32[16,128,256]{1,2,0:T(8,128)}, u32[]{:S(2)}, u32[]{:S(2)}) async-start(f32[16,128,256]{1,2,0:T(8,128)} %bitcast.121), calls=%async_computation | async-start | bytes 4194304 | tf_op jit(solution)/shard_map/all_to_all | solution.py:61
  38.5 2.5 maximum_convert_fusion
  41.0 56.7 %all-to-all-done = f32[16,128,256]{1,2,0:T(8,128)} async-done(((f32[16,128,256]{1,2,0:T(8,128)}), f32[16,128,256]{1,2,0:T(8,128)}, u32[]{:S(2)}, u32[]{:S(2)}) %all-to-all-start) | async-done | bytes 2097184 | tf_op jit(solution)/shard_map/all_to_all | solution.py:61
  97.7 3.5 copy.23
  101.2 72.4 %all-gather.2.cloned.1.call-done = bf16[2048,4096]{1,0:T(8,128)(2,1)} async-done(((bf16[128,4096]{1,0:T(8,128)(2,1)}), bf16[2048,4096]{1,0:T(8,128)(2,1)}) %all-gather.2.cloned.1.call-update) | async-done | bytes 16777232 | tf_op jit(solution)/shard_map/all_gather | solution.py:139
  173.6 9.5 %fusion.82 = f32[256,2048]{1,0:T(8,128)} fusion(bf16[256,4096]{1,0:T(8,128)(2,1)S(1)} %copy-done, bf16[2048,4096]{1,0:T(8,128)(2,1)} %all-gather.2.cloned.1.call-done), kind=kOutput, calls=%fused_computation.202 | convolution fusion | flops 4294967296 | bytes 20971520 | tf_op jit(solution)/shard_map/dot_general | solution.py:141
  183.1 6.8 %multiply_bitcast_fusion = (f32[32,16,8,128]{3,2,1,0:T(8,128)S(1)}, f32[256,2048]{1,0:T(8,128)}) fusion(f32[256,2048]{1,0:T(8,128)} %fusion.82, f32[258,2048]{1,0:T(8,128)} %maximum_convert_fusion, f32[256]{0:T(256)S(1)} %copy-done.30, f32[2048]{0:T(1024)S(1)} %bitcast.143, f32[256]{0:T(256)S(1)} %copy-done.28, f32[2048]{0:T(1024)S(1)} %bitcast.145, ...), kind=kLoop, calls=%fused_computation.65 | loop fusion | flops 4194304 | bytes 12609536
  191.4 5.8 %all-to-all-start.2 = ((f32[16,128,256]{1,2,0:T(8,128)}), f32[16,128,256]{1,2,0:T(8,128)}, u32[]{:S(2)}, u32[]{:S(2)}) async-start(f32[16,128,256]{1,2,0:T(8,128)} %bitcast.120), calls=%async_computation.2 | async-start | bytes 4194304 | tf_op jit(solution)/shard_map/all_to_all | solution.py:61
  197.2 2.8 fusion.4
  203.4 37.0 %all-to-all-done.2 = f32[16,128,256]{1,2,0:T(8,128)} async-done(((f32[16,128,256]{1,2,0:T(8,128)}), f32[16,128,256]{1,2,0:T(8,128)}, u32[]{:S(2)}, u32[]{:S(2)}) %all-to-all-start.2) | async-done | bytes 2097184 | tf_op jit(solution)/shard_map/all_to_all | solution.py:61
  240.5 16.5 %rev.11 = f32[128,32,128]{0,2,1:T(8,128)} reverse(f32[128,32,128]{0,2,1:T(8,128)} %bitcast.32), dimensions={1,2} | reverse | bytes 4194304 | tf_op jit(solution)/shard_map/jit(_flip)/rev | solution.py:72
  259.0 2.8 fusion.7
  265.2 6.8 %multiply_reduce_fusion = (f32[128,32,128]{0,2,1:T(8,128)S(1)}, f32[128,32,128]{0,2,1:T(8,128)}) fusion(f32[2,128,32,128]{1,3,2,0:T(8,128)} %copy-done.5, f32[2,128,32]{1,2,0:T(8,128)S(1)} %pad_multiply_fusion, f32[2,128]{1,0:T(2,128)S(1)} %copy-done.33, f32[2,128,128]{1,2,0:T(8,128)S(1)} %get-tuple-element.90, f32[2,128,32,128]{1,3,2,0:T(8,128)} %copy-done.4, ...), kind=kLoop, calls=%fused_computation.1 | loop fusion | flops 7340032 | bytes 12780544 | tf_op jit(solution)/shard_map/reduce_sum | solution.py:56
  272.0 9.1 %all-to-all-start.1 = ((f32[128,16,256]{0,2,1:T(8,128)}), f32[128,16,256]{0,2,1:T(8,128)}, u32[]{:S(2)}, u32[]{:S(2)}) async-start(f32[128,16,256]{0,2,1:T(8,128)} %bitcast.119), calls=%async_computation.1 | async-start | bytes 4194304 | tf_op jit(solution)/shard_map/all_to_all | solution.py:81
  281.1 10.3 %rev.13 = f32[128,32,128]{0,2,1:T(8,128)} reverse(f32[128,32,128]{0,2,1:T(8,128)S(1)} %get-tuple-element.4), dimensions={1,2} | reverse | bytes 4194304 | tf_op jit(solution)/shard_map/jit(_flip)/rev | solution.py:80
  291.4 33.0 %all-to-all-done.1 = f32[128,16,256]{0,2,1:T(8,128)} async-done(((f32[128,16,256]{0,2,1:T(8,128)}), f32[128,16,256]{0,2,1:T(8,128)}, u32[]{:S(2)}, u32[]{:S(2)}) %all-to-all-start.1) | async-done | bytes 2097184 | tf_op jit(solution)/shard_map/all_to_all | solution.py:81
  324.4 9.3 %all-to-all-start.3 = ((f32[128,16,256]{0,2,1:T(8,128)}), f32[128,16,256]{0,2,1:T(8,128)}, u32[]{:S(2)}, u32[]{:S(2)}) async-start(f32[128,16,256]{0,2,1:T(8,128)} %bitcast.122), calls=%async_computation.3 | async-start | bytes 4194304 | tf_op jit(solution)/shard_map/all_to_all | solution.py:81
  333.8 43.2 %all-to-all-done.3 = f32[128,16,256]{0,2,1:T(8,128)} async-done(((f32[128,16,256]{0,2,1:T(8,128)}), f32[128,16,256]{0,2,1:T(8,128)}, u32[]{:S(2)}, u32[]{:S(2)}) %all-to-all-start.3) | async-done | bytes 2097184 | tf_op jit(solution)/shard_map/all_to_all | solution.py:81
  377.0 5.2 %fusion.64 = (f32[256,2048]{1,0:T(8,128)S(1)}, f32[256,2048]{1,0:T(8,128)S(1)}, f32[256,2048]{1,0:T(8,128)S(1)}, f32[256,2048]{1,0:T(8,128)S(1)}) fusion(f32[256,2048]{1,0:T(8,128)} %get-tuple-element.13, f32[256,2048]{1,0:T(8,128)} %fusion.82, f32[256,2048]{1,0:T(8,128)} %get-tuple-element.18, f32[2048]{0:T(1024)S(1)} %copy-done.31, ...), kind=kLoop, calls=%fused_computation.189 | loop fusion | flops 4194304 | bytes 20979712 | tf_op jit(solution)/shard_map/mul | solution.py:152
  382.6 2.3 collective-permute-start.1
  384.9 11.6 %convolution_convert_fusion = bf16[256,4096]{1,0:T(8,128)(2,1)} fusion(bf16[2048,4096]{1,0:T(8,128)(2,1)} %all-gather.2.cloned.1.call-done, f32[256,2048]{1,0:T(8,128)S(1)} %copy-done.6, f32[256,2048]{1,0:T(8,128)S(1)} %get-tuple-element.20), kind=kOutput, calls=%fused_computation | convolution fusion | flops 4297064448 | bytes 23068672 | tf_op jit(solution)/shard_map/dot_general | solution.py:140
  398.4 4.2 %fusion.14 = (bf16[256,2048]{1,0:T(8,128)(2,1)}, bf16[256,2048]{1,0:T(8,128)(2,1)}) fusion(f32[256,2048]{1,0:T(8,128)S(1)} %mul.732, f32[2,2048]{1,0:T(2,128)S(1)} %get-tuple-element.30, f32[256]{0:T(256)S(1)} %get-tuple-element.71, f32[256]{0:T(256)S(1)} %get-tuple-element.70, f32[2048]{0:T(1024)S(1)} %bitcast.140, f32[2048]{0:T(1024)S(1)} %bitcast.142, ...), kind=kLoop, calls=%fused_computation.19 | loop fusion | flops 10485760 | bytes 6375424 | tf_op jit(solution)/shard_map/convert_element_type | solution.py:164
  (271 shorter events, 31.0 us)
Async XLA Ops:
  7.2 166.4 %copy-start = (bf16[256,4096]{1,0:T(8,128)(2,1)S(1)}, bf16[256,4096]{1,0:T(8,128)(2,1)}, u32[]{:S(2)}) copy-start(bf16[256,4096]{1,0:T(8,128)(2,1)} %param.18) | copy-start | bytes 6291460
  7.2 12.2 %copy-start.7 = (bf16[256,2048]{1,0:T(8,128)(2,1)S(1)}, bf16[256,2048]{1,0:T(8,128)(2,1)}, u32[]{:S(2)}) copy-start(bf16[256,2048]{1,0:T(8,128)(2,1)} %param.11) | copy-start | bytes 3145732
  7.2 166.4 %all-gather.2.cloned.1.call-start = ((), (), s32[]{:S(2)}) async-start(), calls=%async_computation.4 | async-start | bytes 17825792 | tf_op jit(solution)/shard_map/all_gather | solution.py:139
  9.6 9.2 %collective-permute-start = (bf16[3,2,2048]{2,1,0:T(2,128)(2,1)S(1)}, bf16[3,2,2048]{2,1,0:T(2,128)(2,1)S(1)}, u32[]{:S(2)}, u32[]{:S(2)}) collective-permute-start(bf16[3,2,2048]{2,1,0:T(2,128)(2,1)S(1)} %pad_maximum_fusion.3), channel_id=1, source_target_pairs={{0,1},{1,2},{2,3},{3,4},{4,5},{5,6},{6,7},{7,8},{8,9},{9,10},{10,1... | collective-permute-start | bytes 73736 | tf_op jit(solution)/shard_map/ppermute | solution.py:15
  24.7 13.8 %copy-start.9 = (bf16[256,2048]{1,0:T(8,128)(2,1)S(1)}, bf16[256,2048]{1,0:T(8,128)(2,1)}, u32[]{:S(2)}) copy-start(bf16[256,2048]{1,0:T(8,128)(2,1)} %param.10) | copy-start | bytes 3145732
  24.7 73.0 %all-to-all-start = ((f32[16,128,256]{1,2,0:T(8,128)}), f32[16,128,256]{1,2,0:T(8,128)}, u32[]{:S(2)}, u32[]{:S(2)}) async-start(f32[16,128,256]{1,2,0:T(8,128)} %bitcast.121), calls=%async_computation | async-start | bytes 4194304 | tf_op jit(solution)/shard_map/all_to_all | solution.py:61
  101.2 81.9 %copy-start.18 = (f32[1,1,2048]{2,1,0:T(1,128)S(1)}, f32[1,1,2048]{2,1,0:T(1,128)}, u32[]{:S(2)}) copy-start(f32[1,1,2048]{2,1,0:T(1,128)} %get-tuple-element.25) | copy-start | bytes 24580
  101.2 81.9 %copy-start.19 = (f32[1,1,2048]{2,1,0:T(1,128)S(1)}, f32[1,1,2048]{2,1,0:T(1,128)}, u32[]{:S(2)}) copy-start(f32[1,1,2048]{2,1,0:T(1,128)} %get-tuple-element.26) | copy-start | bytes 24580
  101.2 81.9 %copy-start.20 = (f32[1,1,2048]{2,1,0:T(1,128)S(1)}, f32[1,1,2048]{2,1,0:T(1,128)}, u32[]{:S(2)}) copy-start(f32[1,1,2048]{2,1,0:T(1,128)} %get-tuple-element.27) | copy-start | bytes 24580
  101.2 81.9 %copy-start.28 = (f32[256]{0:T(256)S(1)}, f32[256]{0:T(256)}, u32[]{:S(2)}) copy-start(f32[256]{0:T(256)} %copy-done.27) | copy-start | bytes 3076
  101.2 81.9 %copy-start.30 = (f32[256]{0:T(256)S(1)}, f32[256]{0:T(256)}, u32[]{:S(2)}) copy-start(f32[256]{0:T(256)} %copy-done.29) | copy-start | bytes 3076
  191.4 49.1 %all-to-all-start.2 = ((f32[16,128,256]{1,2,0:T(8,128)}), f32[16,128,256]{1,2,0:T(8,128)}, u32[]{:S(2)}, u32[]{:S(2)}) async-start(f32[16,128,256]{1,2,0:T(8,128)} %bitcast.120), calls=%async_computation.2 | async-start | bytes 4194304 | tf_op jit(solution)/shard_map/all_to_all | solution.py:61
  197.2 6.0 %copy-start.26 = (f32[2,128,15]{1,2,0:T(8,128)S(1)}, f32[2,128,15]{1,2,0:T(8,128)}, u32[]{:S(2)}) copy-start(f32[2,128,15]{1,2,0:T(8,128)} %slice.510) | copy-start | bytes 46084
  197.2 6.0 %copy-start.35 = (f32[2,128,1]{1,2,0:T(1,128)S(1)}, f32[2,128,1]{1,2,0:T(1,128)}, u32[]{:S(2)}) copy-start(f32[2,128,1]{1,2,0:T(1,128)} %slice.607) | copy-start | bytes 3076
  197.2 6.2 %copy-start.39 = (f32[32]{0:T(128)S(1)}, f32[32]{0:T(128)}, u32[]{:S(2)}) copy-start(f32[32]{0:T(128)} %copy-done.38) | copy-start | bytes 388
  259.0 6.0 %copy-start.34 = (f32[2,128,1]{1,2,0:T(1,128)S(1)}, f32[2,128,1]{1,2,0:T(1,128)}, u32[]{:S(2)}) copy-start(f32[2,128,1]{1,2,0:T(1,128)} %slice.639) | copy-start | bytes 3076
  259.0 6.1 %copy-start.37 = (f32[32]{0:T(128)S(1)}, f32[32]{0:T(128)}, u32[]{:S(2)}) copy-start(f32[32]{0:T(128)} %copy-done.36) | copy-start | bytes 388
  259.0 6.2 %copy-start.33 = (f32[2,128]{1,0:T(2,128)S(1)}, f32[2,128]{1,0:T(2,128)}, u32[]{:S(2)}) copy-start(f32[2,128]{1,0:T(2,128)} %get-tuple-element.15) | copy-start | bytes 3076
  272.0 52.4 %all-to-all-start.1 = ((f32[128,16,256]{0,2,1:T(8,128)}), f32[128,16,256]{0,2,1:T(8,128)}, u32[]{:S(2)}, u32[]{:S(2)}) async-start(f32[128,16,256]{0,2,1:T(8,128)} %bitcast.119), calls=%async_computation.1 | async-start | bytes 4194304 | tf_op jit(solution)/shard_map/all_to_all | solution.py:81
  324.4 9.3 %copy-start.32 = (f32[384]{0:T(512)S(1)}, f32[384]{0:T(512)}, u32[]{:S(2)}) copy-start(f32[384]{0:T(512)} %get-tuple-element.86) | copy-start | bytes 4612
  324.4 52.6 %copy-start.3 = (f32[256,2048]{1,0:T(8,128)S(1)}, f32[256,2048]{1,0:T(8,128)}, u32[]{:S(2)}) copy-start(f32[256,2048]{1,0:T(8,128)} %get-tuple-element.14) | copy-start | bytes 6291460
  324.4 52.6 %copy-start.31 = (f32[2048]{0:T(1024)S(1)}, f32[2048]{0:T(1024)}, u32[]{:S(2)}) copy-start(f32[2048]{0:T(1024)} %param.16) | copy-start | bytes 24580
  324.4 52.6 %all-to-all-start.3 = ((f32[128,16,256]{0,2,1:T(8,128)}), f32[128,16,256]{0,2,1:T(8,128)}, u32[]{:S(2)}, u32[]{:S(2)}) async-start(f32[128,16,256]{0,2,1:T(8,128)} %bitcast.122), calls=%async_computation.3 | async-start | bytes 4194304 | tf_op jit(solution)/shard_map/all_to_all | solution.py:81
  382.6 13.9 %collective-permute-start.1 = (bf16[3,2,2048]{2,1,0:T(2,128)(2,1)S(1)}, bf16[3,2,2048]{2,1,0:T(2,128)(2,1)S(1)}, u32[]{:S(2)}, u32[]{:S(2)}) collective-permute-start(bf16[3,2,2048]{2,1,0:T(2,128)(2,1)S(1)} %pad_maximum_fusion.4), channel_id=1, source_target_pairs={{1,0},{2,1},{3,2},{4,3},{5,4},{6,5},{7,6},{8,7},{9,8},{10,9},{11,1... | collective-permute-start | bytes 73736 | tf_op jit(solution)/shard_map/ppermute | solution.py:15
  (23 other events, 74.8 us)
Sparse Core Ops, SparseCore 0:
  10.2 163.3 all-gather.1
where the time goes:
time: 416 us; the launch traced here: 409 us
  waiting for transfers between devices  243 us (58%)
  local copies, waits for them, and re-layouts  50.3 us (12%)
  other arithmetic  38.9 us (9%)
  starting transfers between devices  35.5 us (9%)
  matrix products  26.6 us (6%)
  between operations  15.2 us (4%)
    all_to_all x2, waiting for transfers between devices, relay_pass(): lax.all_to_all(columns, 'seq', split_axis=0, concat_axis=1, tiled=True)  93.7 us
    all_to_all x2, waiting for transfers between devices, relay_pass(): lax.all_to_all(result.reshape(share_width, block_count * BLOCK), 'seq', s...  76.2 us
    all_gather x1, waiting for transfers between devices, on_device(): weight_piece = lax.all_gather(out_weight, 'seq', axis=0, tiled=True)  72.4 us
    rev x2, local copies, waits for them, and re-layouts, relay_pass(): blocked = jnp.flip(blocked, axis=(1, 2))  18.5 us
    all_to_all x2, starting transfers between devices, relay_pass(): lax.all_to_all(result.reshape(share_width, block_count * BLOCK), 'seq', s...  18.4 us
    dot_general x1, matrix products, on_device(): jnp.dot(gated_rows, weight_piece, preferred_element_type=jnp.float32)  11.6 us
    all_to_all x2, starting transfers between devices, relay_pass(): lax.all_to_all(columns, 'seq', split_axis=0, concat_axis=1, tiled=True)  11 us
    rev x1, local copies, waits for them, and re-layouts, relay_pass(): result = jnp.flip(result, axis=(1, 2))  10.3 us
  transfers between devices with their start and end apart: 7, of which 5 were waited for; matrix products, arithmetic and copies ran while one was open for 13% of the time, Pallas kernels for 0%

commit v1 on v0

v1 whole, which is shorter than its diff:
```python
import functools

import jax
import jax.numpy as jnp
from jax import lax
from jax.experimental import pallas as pl
from jax.experimental.pallas import tpu as pltpu
from jax.sharding import PartitionSpec as P

BLOCK = 128
REACH = 8
Z_SIZE = 4
MESH_ID = pl.DeviceIdType.MESH
ROUTES = (("zxy", 7), ("zyx", 6), ("xyz", 3))
F32 = jnp.float32
BF16 = jnp.bfloat16


def last_axis(order, dz, dx, dy):
    moved = {"z": dz != 0, "x": dx != 0, "y": dy != 0}
    if dz == 0 and dx == 0:
        return -1 if dy == 0 else order.index("y")
    return max(i for i in range(3) if moved[order[i]])


def sends_of(order, dz, dx, dy):
    last = last_axis(order, dz, dx, dy)
    moves = []
    for i in range(3):
        axis = order[i]
        if i < last or (i == last and axis != "z"):
            continue
        if axis == "z":
            if dz >= 0:
                moves.append("up")
            if dz <= 0:
                moves.append("down")
        elif axis == "x":
            moves.append("x")
        elif not (dz == 0 and dx == 0):
            moves.append("y")
    return moves


def all_sites():
    sites = []
    for dz in range(-(Z_SIZE - 1), Z_SIZE):
        for dx in range(2):
            for dy in range(2):
                for r in range(len(ROUTES)):
                    sites.append((abs(dz) + dx + dy, dz, dx, dy, r))
    return sorted(sites)


def send_slots():
    slots = {}
    for _, dz, dx, dy, r in all_sites():
        for move in sends_of(ROUTES[r][0], dz, dx, dy):
            slots.setdefault((r, dx, dy, move), len(slots))
    return slots


def scan_down(x, rates):
    rows = x.shape[0]
    row = lax.broadcasted_iota(jnp.int32, x.shape, 0)
    step = 1
    while step < rows:
        factor = jnp.exp(-rates * float(step))
        if step < 8:
            moved = jnp.where(row >= step, pltpu.roll(x, step, 0), 0.0)
        else:
            moved = jnp.concatenate([jnp.zeros((step, x.shape[1]), F32), x[: rows - step]], axis=0)
        x = x + factor * moved
        step *= 2
    return x


def scan_up(x, rates):
    rows = x.shape[0]
    row = lax.broadcasted_iota(jnp.int32, x.shape, 0)
    step = 1
    while step < rows:
        factor = jnp.exp(-rates * float(step))
        if step < 8:
            moved = jnp.where(row < rows - step, pltpu.roll(x, rows - step, 0), 0.0)
        else:
            moved = jnp.concatenate([x[step:], jnp.zeros((step, x.shape[1]), F32)], axis=0)
        x = x + factor * moved
        step *= 2
    return x


def kernel(
    seq, gathers, docs_ref, q_ref, k_ref, v_ref, taps_ref, rates_ref, res_ref, skip_ref, w_ref, cot_ref,
    out_ref, gq_ref, gk_ref, gv_ref,
    wbuf, qs, ks, vs, conv, gated, acc, gqs, gp, edge, gsend, gedge, e_own, e_in, b_own, b_in,
    edge_sems, gedge_sems, e_sems, b_sems, local_sem, recv_sems, send_sems, core_sems, full_sems,
):
    me = lax.axis_index("seq")
    grp = lax.axis_index("groups")
    rows = q_ref.shape[0]
    chan = q_ref.shape[1]
    width = 256
    half_cols = cot_ref.shape[1] // 2
    piece_rows = w_ref.shape[0]
    per_dev = rows // BLOCK
    z, x, core = me // 4, (me // 2) % 2, me % 2

    starts = [jnp.int32(0)]
    for i in range(docs_ref.shape[0]):
        starts.append(starts[-1] + docs_ref[i])

    def free(low, high):
        kept = jnp.float32(1.0)
        for start in starts:
            kept = jnp.where((start >= low) & (start < high), 0.0, kept)
        return kept

    first = me * per_dev
    keep_0, keep_1, keep_n = free(first, first + 1), free(first + 1, first + 2), free(first + 2, first + 3)

    barrier = pltpu.get_barrier_semaphore()
    greeted = jnp.int32(0)
    for k in range(1, REACH + 1):
        for other in (me + k, me - k):
            there = (other >= 0) & (other < seq)

            @pl.when(there)
            def _():
                pl.semaphore_signal(barrier, inc=1, device_id=(grp, other), device_id_type=MESH_ID)

            greeted = greeted + there.astype(jnp.int32)
    if gathers:
        pl.semaphore_signal(barrier, inc=1, device_id=(1 - grp, me), device_id_type=MESH_ID)
        greeted = greeted + 1
    pl.semaphore_wait(barrier, greeted)

    def edge_copy(i, ref, target):
        return pltpu.make_async_remote_copy(
            src_ref=ref.at[pl.ds(rows - 16, 16)], dst_ref=edge.at[i], send_sem=edge_sems.at[i],
            recv_sem=edge_sems.at[3 + i], device_id=(grp, target), device_id_type=MESH_ID)

    @pl.when(me + 1 < seq)
    def _():
        for i, ref in enumerate((q_ref, k_ref, v_ref)):
            edge_copy(i, ref, me + 1).start()

    @pl.when(me == 0)
    def _():
        edge[...] = jnp.zeros_like(edge)

    offsets, at = [], 0
    for _, share in ROUTES:
        offsets.append((at * half_cols // 16, share * half_cols // 16))
        at += share
    slots = send_slots()

    def part(r, z_at, x_at, y_at, c_at):
        start, size = offsets[r]
        col = pl.multiple_of(y_at * half_cols + start, 128)
        return wbuf.at[z_at * 2 + x_at, pl.ds(pl.multiple_of(c_at * piece_rows, 16), piece_rows), pl.ds(col, size)]

    def own_rows(c_at):
        return wbuf.at[z * 2 + x, pl.ds(pl.multiple_of(c_at * piece_rows, 16), piece_rows)]

    def flat(r, dx, dy):
        return (r * 2 + dx) * 2 + dy

    def hop(r, z_at, dx, dy, move):
        ref = part(r, z_at, x ^ dx, grp ^ dy, core)
        to = {"up": (grp, me + 4), "down": (grp, me - 4), "x": (grp, me ^ 2), "y": (1 - grp, me)}[move]
        there = flat(r, dx ^ 1 if move == "x" else dx, dy ^ 1 if move == "y" else dy)
        return pltpu.make_async_remote_copy(
            src_ref=ref, dst_ref=ref, send_sem=send_sems.at[slots[(r, dx, dy, move)] * Z_SIZE + z_at],
            recv_sem=recv_sems.at[there * Z_SIZE + z_at], device_id=to, device_id_type=MESH_ID)

    def share_core(r, z_at, dx, dy, c_at):
        ref = part(r, z_at, x ^ dx, grp ^ dy, c_at)
        index = flat(r, dx, dy) * Z_SIZE + z_at
        return pltpu.make_async_remote_copy(
            src_ref=ref, dst_ref=ref, send_sem=core_sems.at[0, index], recv_sem=core_sems.at[1, index],
            device_id=(grp, me ^ 1), device_id_type=MESH_ID)

    def share_full(c_at):
        return pltpu.make_async_remote_copy(
            src_ref=own_rows(c_at), dst_ref=own_rows(c_at), send_sem=full_sems.at[0], recv_sem=full_sems.at[1],
            device_id=(grp, me ^ 1), device_id_type=MESH_ID)

    def when_valid(dz, action):
        z_at = z - dz
        if dz == 0:
            action(z)
        else:
            @pl.when((z_at >= 0) & (z_at < Z_SIZE))
            def _():
                action(z_at)

    def when_move(move, action):
        if move == "up":
            pl.when(z + 1 < Z_SIZE)(action)
        elif move == "down":
            pl.when(z > 0)(action)
        else:
            action()

    def visit(dz, dx, dy, r):
        def action(z_at):
            if dz != 0 or dx != 0:
                ref = part(r, z_at, x ^ dx, grp ^ dy, core)
                sem = recv_sems.at[flat(r, dx, dy) * Z_SIZE + z_at]
                pltpu.make_async_remote_copy(
                    src_ref=ref, dst_ref=ref, send_sem=sem, recv_sem=sem,
                    device_id=(grp, me ^ 1), device_id_type=MESH_ID).wait_recv()
            for move in sends_of(ROUTES[r][0], dz, dx, dy):
                when_move(move, lambda move=move: hop(r, z_at, dx, dy, move).start())
            if dz != 0 or dx != 0:
                share_core(r, z_at, dx, dy, core).start()
        when_valid(dz, action)

    sites = all_sites()
    if gathers:
        local = pltpu.make_async_copy(w_ref, own_rows(core), local_sem)
        local.start()
        local.wait()
        for _, dz, dx, dy, r in sites:
            if dz == 0 and dx == 0:
                visit(dz, dx, dy, r)
        share_full(core).start()
    else:
        local = pltpu.make_async_copy(w_ref, wbuf, local_sem)
        local.start()

    def columns(i):
        return pl.ds(pl.multiple_of(i * width, width), width)

    row = lax.broadcasted_iota(jnp.int32, (rows, width), 0)
    block_row = lax.broadcasted_iota(jnp.int32, (BLOCK, width), 0).astype(F32)

    def weights_of(cols):
        rates = rates_ref[:, cols]
        return rates, res_ref[:, cols] * jnp.sqrt(2.0 * rates)

    lag_1 = jnp.where(row == 0, keep_0, jnp.where(row == BLOCK, keep_1, 1.0))
    lag_2 = jnp.where(row < 2, keep_0, jnp.where((row == BLOCK) | (row == BLOCK + 1), keep_1, 1.0))

    @pl.when(me > 0)
    def _():
        for i, ref in enumerate((q_ref, k_ref, v_ref)):
            edge_copy(i, ref, me).wait_recv()

    def forward_chunk(i, carry):
        cols = columns(i)

        def short(b, ref):
            now = ref[:, cols].astype(F32)
            before = edge[b, :, cols].astype(F32)
            one = jnp.where(row == 0, before[15:16], pltpu.roll(now, 1, 0))
            two = jnp.where(row == 0, before[14:15], jnp.where(row == 1, before[15:16], pltpu.roll(now, 2, 0)))
            return (taps_ref[b, 0:1, cols] * now + taps_ref[b, 1:2, cols] * (lag_1 * one)
                    + taps_ref[b, 2:3, cols] * (lag_2 * two))

        qs[:, cols] = short(0, q_ref)
        k_now, v_now = short(1, k_ref), short(2, v_ref)
        ks[:, cols] = k_now
        vs[:, cols] = v_now
        product = k_now * v_now
        rates, weight = weights_of(cols)
        skip = skip_ref[:, cols]
        top, low = skip * product[:BLOCK], skip * product[BLOCK:]
        for m in range(2):
            rate = rates[m : m + 1]
            y_0 = scan_down(product[:BLOCK], rate)
            y_1 = scan_down(product[BLOCK:], rate)
            y_1 = y_1 + jnp.exp(-rate * (block_row + 1.0)) * (keep_1 * y_0[BLOCK - 1 :])
            e_own[m : m + 1, cols] = y_1[BLOCK - 1 :]
            top = top + weight[m : m + 1] * y_0
            low = low + weight[m : m + 1] * y_1
        conv[:BLOCK, cols] = top
        conv[BLOCK:, cols] = low
        return carry

    lax.fori_loop(0, chan // width, forward_chunk, 0)

    def state_copy(own, into, sems, k, target):
        return pltpu.make_async_remote_copy(
            src_ref=own, dst_ref=into.at[k - 1], send_sem=sems.at[0, k - 1], recv_sem=sems.at[1, k - 1],
            device_id=(grp, target), device_id_type=MESH_ID)

    def send_states(own, into, sems, sign):
        for k in range(1, REACH + 1):
            @pl.when((me + sign * k >= 0) & (me + sign * k < seq))
            def _():
                state_copy(own, into, sems, k, me + sign * k).start()

    def take_states(own, into, sems, sign):
        for k in range(1, REACH + 1):
            there = (me - sign * k >= 0) & (me - sign * k < seq)

            @pl.when(there)
            def _():
                state_copy(own, into, sems, k, me).wait_recv()

            @pl.when(jnp.logical_not(there))
            def _():
                into[k - 1] = jnp.zeros_like(into[k - 1])

    def joined(into, rates, cols, kept):
        total = jnp.zeros_like(rates)
        for k in range(1, REACH + 1):
            total = total + into[k - 1, :, cols] * jnp.exp(-rates * float(rows * (k - 1))) * kept[k - 1]
        return total

    send_states(e_own, e_in, e_sems, 1)
    if gathers:
        for level, dz, dx, dy, r in sites:
            if level == 1 and (dz != 0 or dx != 0):
                visit(dz, dx, dy, r)
    take_states(e_own, e_in, e_sems, 1)
    kept_f = [free(per_dev * (me - k + 1), first) for k in range(1, REACH + 1)]
    kept_b = [free(first + per_dev + 1, first + per_dev * k + 1) for k in range(1, REACH + 1)]

    def forward_finish(i, carry):
        cols = columns(i)
        rates, weight = weights_of(cols)
        ahead = joined(e_in, rates, cols, kept_f) * weight * keep_0
        later = ahead * keep_1 * jnp.exp(-rates * float(BLOCK))
        top, low = conv[:BLOCK, cols], conv[BLOCK:, cols]
        for m in range(2):
            power = jnp.exp(-rates[m : m + 1] * (block_row + 1.0))
            top = top + power * ahead[m : m + 1]
            low = low + power * later[m : m + 1]
        conv[:BLOCK, cols] = top
        conv[BLOCK:, cols] = low
        gated[:BLOCK, cols] = (qs[:BLOCK, cols] * top).astype(BF16)
        gated[BLOCK:, cols] = (qs[BLOCK:, cols] * low).astype(BF16)
        return carry

    lax.fori_loop(0, chan // width, forward_finish, 0)
    acc[...] = jnp.zeros_like(acc)

    tile = 512

    def multiply(j):
        cols = columns(j)
        grad = lax.dot_general(cot_ref[...], wbuf[j], (((1,), (1,)), ((), ())), preferred_element_type=F32)
        gqs[:, cols] = grad * conv[:, cols]
        grad_conv = grad * qs[:, cols]
        rates, weight = weights_of(cols)
        skip = skip_ref[:, cols]
        top, low = skip * grad_conv[:BLOCK], skip * grad_conv[BLOCK:]
        for m in range(2):
            rate = rates[m : m + 1]
            y_0 = scan_up(grad_conv[:BLOCK], rate)
            y_1 = scan_up(grad_conv[BLOCK:], rate)
            y_0 = y_0 + jnp.exp(-rate * (BLOCK - block_row)) * (keep_1 * y_1[0:1])
            b_own[m : m + 1, cols] = y_0[0:1]
            top = top + weight[m : m + 1] * y_0
            low = low + weight[m : m + 1] * y_1
        gp[:BLOCK, cols] = top
        gp[BLOCK:, cols] = low

        def mixed(t, carry):
            at = pl.ds(pl.multiple_of(t * tile, tile), tile)
            acc[:, at] = acc[:, at] + jnp.dot(gated[:, cols], wbuf[j, :, at], preferred_element_type=F32)
            return carry

        lax.fori_loop(0, acc.shape[1] // tile, mixed, 0)

    def settle(dz, dx):
        def action(z_at):
            if dz == 0 and dx == 0:
                share_full(1 - core).wait_recv()
            else:
                for dy in range(2):
                    for r in range(len(ROUTES)):
                        share_core(r, z_at, dx, dy, 1 - core).wait_recv()
            multiply(z_at * 2 + (x ^ dx))
        when_valid(dz, action)

    if gathers:
        top_level = max(site[0] for site in sites)
        pairs = sorted((abs(dz) + dx + 1, dz, dx) for dz in range(1 - Z_SIZE, Z_SIZE) for dx in range(2))
        for level in range(2, top_level + 2):
            for site_level, dz, dx, dy, r in sites:
                if site_level == level and (dz != 0 or dx != 0):
                    visit(dz, dx, dy, r)
            for pair_level, dz, dx in pairs:
                if pair_level == level - 1:
                    settle(dz, dx)
        for pair_level, dz, dx in pairs:
            if pair_level > top_level:
                settle(dz, dx)
    else:
        local.wait()

        def each(j, carry):
            multiply(j)
            return carry

        lax.fori_loop(0, chan // width, each, 0)

    send_states(b_own, b_in, b_sems, -1)

    def write_mixed(t, carry):
        at = pl.ds(pl.multiple_of(t * tile, tile), tile)
        out_ref[:, at] = acc[:, at].astype(BF16)
        return carry

    lax.fori_loop(0, acc.shape[1] // tile, write_mixed, 0)
    take_states(b_own, b_in, b_sems, -1)

    def backward_finish(i, carry):
        cols = columns(i)
        rates, weight = weights_of(cols)
        behind = joined(b_in, rates, cols, kept_b) * weight * keep_n
        sooner = behind * keep_1 * jnp.exp(-rates * float(BLOCK))
        top, low = gp[:BLOCK, cols], gp[BLOCK:, cols]
        for m in range(2):
            power = jnp.exp(-rates[m : m + 1] * (BLOCK - block_row))
            top = top + power * sooner[m : m + 1]
            low = low + power * behind[m : m + 1]
        grad = jnp.concatenate([top, low], axis=0)
        k_now = ks[:, cols]
        grad_k, grad_v = grad * vs[:, cols], grad * k_now
        ks[:, cols] = grad_k
        vs[:, cols] = grad_v
        gsend[0, :, cols] = gqs[0:8, cols]
        gsend[1, :, cols] = grad_k[0:8]
        gsend[2, :, cols] = grad_v[0:8]
        return carry

    lax.fori_loop(0, chan // width, backward_finish, 0)

    def gedge_copy(target):
        return pltpu.make_async_remote_copy(
            src_ref=gsend, dst_ref=gedge, send_sem=gedge_sems.at[0], recv_sem=gedge_sems.at[1],
            device_id=(grp, target), device_id_type=MESH_ID)

    @pl.when(me > 0)
    def _():
        gedge_copy(me - 1).start()

    @pl.when(me == seq - 1)
    def _():
        gedge[...] = jnp.zeros_like(gedge)

    @pl.when(me + 1 < seq)
    def _():
        gedge_copy(me).wait_recv()

    lead_1 = jnp.where(row == BLOCK - 1, keep_1, jnp.where(row == rows - 1, keep_n, 1.0))
    lead_2 = jnp.where((row == BLOCK - 1) | (row == BLOCK - 2), keep_1, jnp.where(row >= rows - 2, keep_n, 1.0))

    def backward_short(i, carry):
        cols = columns(i)
        for b, (grad_ref, to_ref) in enumerate(((gqs, gq_ref), (ks, gk_ref), (vs, gv_ref))):
            now = grad_ref[:, cols]
            after = gedge[b, :, cols]
            one = jnp.where(row == rows - 1, after[0:1], pltpu.roll(now, rows - 1, 0))
            two = jnp.where(row == rows - 1, after[1:2],
                            jnp.where(row == rows - 2, after[0:1], pltpu.roll(now, rows - 2, 0)))
            to_ref[:, cols] = (taps_ref[b, 0:1, cols] * now + taps_ref[b, 1:2, cols] * (lead_1 * one)
                               + taps_ref[b, 2:3, cols] * (lead_2 * two)).astype(BF16)
        return carry

    lax.fori_loop(0, chan // width, backward_short, 0)

    @pl.when(me + 1 < seq)
    def _():
        for i, ref in enumerate((q_ref, k_ref, v_ref)):
            edge_copy(i, ref, me + 1).wait_send()

    @pl.when(me > 0)
    def _():
        gedge_copy(me - 1).wait_send()

    for own, into, sems, sign in ((e_own, e_in, e_sems, 1), (b_own, b_in, b_sems, -1)):
        for k in range(1, REACH + 1):
            @pl.when((me + sign * k >= 0) & (me + sign * k < seq))
            def _():
                state_copy(own, into, sems, k, me + sign * k).wait_send()

    if gathers:
        share_full(core).wait_send()
        for _, dz, dx, dy, r in sites:
            def action(z_at):
                for move in sends_of(ROUTES[r][0], dz, dx, dy):
                    when_move(move, lambda move=move: hop(r, z_at, dx, dy, move).wait_send())
                if dz != 0 or dx != 0:
                    share_core(r, z_at, dx, dy, core).wait_send()
            when_valid(dz, action)


def on_device(queries, key_inputs, values, short_taps, decay_rates, residues, skip_gain, out_weight, cotangent,
              doc_blocks):
    seq = lax.axis_size("seq")
    rows, chan = queries.shape
    model = out_weight.shape[1]
    gathers = seq == 4 * Z_SIZE and lax.axis_size("groups") == 2
    pairs = chan // 256
    if not gathers:
        out_weight = lax.all_gather(out_weight, "seq", axis=0, tiled=True).reshape(pairs, 256, model)
    vmem = pl.BlockSpec(memory_space=pltpu.VMEM)
    dma = pltpu.SemaphoreType.DMA
    count = len(ROUTES) * 4 * Z_SIZE
    full = (rows, chan)
    return pl.pallas_call(
        functools.partial(kernel, seq, gathers),
        out_shape=(
            jax.ShapeDtypeStruct((rows, model), BF16),
            jax.ShapeDtypeStruct(full, BF16),
            jax.ShapeDtypeStruct(full, BF16),
            jax.ShapeDtypeStruct(full, BF16),
        ),
        in_specs=[pl.BlockSpec(memory_space=pltpu.SMEM)] + [vmem] * 7
        + [pl.BlockSpec(memory_space=pl.ANY)] + [vmem],
        out_specs=(vmem,) * 4,
        scratch_shapes=[
            pltpu.VMEM((pairs, 256, model), BF16),
            pltpu.VMEM(full, F32), pltpu.VMEM(full, F32), pltpu.VMEM(full, F32), pltpu.VMEM(full, F32),
            pltpu.VMEM(full, BF16),
            pltpu.VMEM((rows, model), F32),
            pltpu.VMEM(full, F32), pltpu.VMEM(full, F32),
            pltpu.VMEM((3, 16, chan), BF16),
            pltpu.VMEM((3, 8, chan), F32), pltpu.VMEM((3, 8, chan), F32),
            pltpu.VMEM((2, chan), F32), pltpu.VMEM((REACH, 2, chan), F32),
            pltpu.VMEM((2, chan), F32), pltpu.VMEM((REACH, 2, chan), F32),
            dma((6,)), dma((2,)), dma((2, REACH)), dma((2, REACH)), dma,
            dma((count,)), dma((len(send_slots()) * Z_SIZE,)), dma((2, count)), dma((2,)),
        ],
        compiler_params=pltpu.CompilerParams(
            collective_id=0, has_side_effects=True, vmem_limit_bytes=60 * 1024 * 1024),
    )(doc_blocks, queries, key_inputs, values, short_taps, decay_rates, residues, skip_gain.reshape(1, chan),
      out_weight, cotangent)


def solution(mesh):
    rows = P(("groups", "seq"), None)
    return jax.shard_map(
        on_device,
        mesh=mesh,
        in_specs=(rows, rows, rows, P(), P(), P(), P(), P("seq", None), rows, P("groups")),
        out_specs=(rows, rows, rows, rows),
        check_vma=False,
    )
```

time: 416 us -> 112 us (0.27); the launches traced: 409 us -> 110 us
  waiting for transfers between devices: 243 us -> 0 us
  Pallas kernels: 0 us -> 103 us
  local copies, waits for them, and re-layouts: 50.3 us -> 6.2 us
  other arithmetic: 38.9 us -> 0 us
  starting transfers between devices: 35.5 us -> 0 us
  matrix products: 26.6 us -> 0 us
  between operations: 15.2 us -> 0.66 us
    all_to_all x4 -> x0, waiting for transfers between devices: 170 us -> none  [the longest x2 93.7 us: relay_pass(): lax.all_to_all(columns, 'seq', split_axis=0, concat_axis=1, tiled=True)]
    pallas_call x0 -> x1, Pallas kernels: none -> 103 us  [on_device(): pl.pallas_call(functools.partial(kernel, seq, gathers), out_shape=(jax.Sh...]
    all_gather x1 -> x0, waiting for transfers between devices: 72.4 us -> none  [on_device(): weight_piece = lax.all_gather(out_weight, 'seq', axis=0, tiled=True)]
    all_to_all x4 -> x0, starting transfers between devices: 29.4 us -> none  [the longest x2 18.4 us: relay_pass(): lax.all_to_all(result.reshape(share_width, block_count * BLOCK), 'seq', s...]
    rev x4 -> x0, local copies, waits for them, and re-layouts: 28.8 us -> none  [the longest x2 18.5 us: relay_pass(): blocked = jnp.flip(blocked, axis=(1, 2))]
    dot_general x4 -> x0, matrix products: 26.6 us -> none  [the longest x1 11.6 us: on_device(): jnp.dot(gated_rows, weight_piece, preferred_element_type=jnp.float32)]
    unnamed x2 -> x0, other arithmetic: 9.89 us -> none
    convert_element_type x9 -> x0, other arithmetic: 9.24 us -> none  [the longest x2 6.11 us: backward_short(): return summed.astype(jnp.bfloat16)]
  transfers between devices with their start and end apart: 7 -> 0, of which waited for: 5 -> 0; matrix products, arithmetic and copies ran while one was open for 13% -> 0% of each run, Pallas kernels for 0% -> 0%
where the time goes in v1:
time: 112 us; the launch traced here: 110 us
  Pallas kernels  103 us (92%)
  local copies, waits for them, and re-layouts  6.2 us (6%)
    pallas_call x1, Pallas kernels, on_device(): pl.pallas_call(functools.partial(kernel, seq, gathers), out_shape=(jax.Sh...  103 us
    unnamed x10, local copies, waits for them, and re-layouts  6.2 us

profile of v1, /device:TPU:3, one launch (start us, length us, event | category | flops | bytes accessed | tf_op | source)
XLA Modules:
  0.0 109.9 jit_solution(8073051030528686588)
XLA Ops:
  0.6 103.1 %shard_map.129 = (bf16[256,4096]{1,0:T(8,128)(2,1)}, bf16[256,2048]{1,0:T(8,128)(2,1)}, bf16[256,2048]{1,0:T(8,128)(2,1)}, bf16[256,2048]{1,0:T(8,128)(2,1)}) custom-call(s32[4]{0:T(128)} %docs_ref.1, bf16[256,2048]{1,0:T(8,128)(2,1)} %q_ref.1, bf16[256,2048]{1,0:T(8,128)(2,1)} %k_ref.1, bf16[256,2048]{1,0:T(8,128)(2,1)} %v_ref.1, f32[3,3,2048]{2,1,0:T(4,128)} %taps_ref.1, ...), custom_call_target="tpu_custom_call" | custom-call | tf_op jit(solution)/shard_map/pallas_call | solution.py:507
  103.7 0.0 copy-start.2
  103.7 0.0 copy-start.1
  103.7 3.3 %copy.18 = bf16[256,4096]{1,0:T(8,128)(2,1)} copy(bf16[256,4096]{1,0:T(8,128)(2,1)} %get-tuple-element.8) | data formatting | bytes 4194304
  107.0 0.0 copy-done.2
  107.0 0.0 copy-start
  107.0 1.0 copy.19
  108.0 0.0 copy-done.1
  108.0 1.0 copy.20
  109.0 0.0 copy-done
  109.0 1.0 copy.21
Async XLA Ops:
  103.7 3.3 %copy-start.2 = (bf16[256,2048]{1,0:T(8,128)(2,1)S(1)}, bf16[256,2048]{1,0:T(8,128)(2,1)}, u32[]{:S(2)}) copy-start(bf16[256,2048]{1,0:T(8,128)(2,1)} %get-tuple-element.9) | copy-start | bytes 3145732
  103.7 4.3 %copy-start.1 = (bf16[256,2048]{1,0:T(8,128)(2,1)S(1)}, bf16[256,2048]{1,0:T(8,128)(2,1)}, u32[]{:S(2)}) copy-start(bf16[256,2048]{1,0:T(8,128)(2,1)} %get-tuple-element.10) | copy-start | bytes 3145732
  107.0 1.9 %copy-start = (bf16[256,2048]{1,0:T(8,128)(2,1)S(1)}, bf16[256,2048]{1,0:T(8,128)(2,1)}, u32[]{:S(2)}) copy-start(bf16[256,2048]{1,0:T(8,128)(2,1)} %get-tuple-element.11) | copy-start | bytes 3145732

commit v2 on v1

--- a/solution.py
+++ b/solution.py
@@ -91,10 +91,11 @@
 
 
 def kernel(
-    seq, gathers, docs_ref, q_ref, k_ref, v_ref, taps_ref, rates_ref, res_ref, skip_ref, w_ref, cot_ref,
-    out_ref, gq_ref, gk_ref, gv_ref,
+    seq, gathers, docs_ref, q_hbm, k_hbm, v_hbm, taps_ref, rates_ref, res_ref, skip_ref, w_ref, cot_hbm,
+    out_hbm, gq_hbm, gk_hbm, gv_hbm,
+    q_ref, k_ref, v_ref, cot_ref, out_ref, gq_ref, gk_ref, gv_ref,
     wbuf, qs, ks, vs, conv, gated, acc, gqs, gp, edge, gsend, gedge, e_own, e_in, b_own, b_in,
-    edge_sems, gedge_sems, e_sems, b_sems, local_sem, recv_sems, send_sems, core_sems, full_sems,
+    edge_sems, gedge_sems, e_sems, b_sems, local_sem, recv_sems, send_sems, core_sems, full_sems, in_sems, out_sems,
 ):
     me = lax.axis_index("seq")
     grp = lax.axis_index("groups")
@@ -119,6 +120,11 @@
     first = me * per_dev
     keep_0, keep_1, keep_n = free(first, first + 1), free(first + 1, first + 2), free(first + 2, first + 3)
 
+    loads = [pltpu.make_async_copy(a, b, in_sems.at[i]) for i, (a, b) in enumerate(
+        ((q_hbm, q_ref), (k_hbm, k_ref), (v_hbm, v_ref), (cot_hbm, cot_ref)))]
+    for load in loads:
+        load.start()
+
     barrier = pltpu.get_barrier_semaphore()
     greeted = jnp.int32(0)
     for k in range(1, REACH + 1):
@@ -140,15 +146,6 @@
             src_ref=ref.at[pl.ds(rows - 16, 16)], dst_ref=edge.at[i], send_sem=edge_sems.at[i],
             recv_sem=edge_sems.at[3 + i], device_id=(grp, target), device_id_type=MESH_ID)
 
-    @pl.when(me + 1 < seq)
-    def _():
-        for i, ref in enumerate((q_ref, k_ref, v_ref)):
-            edge_copy(i, ref, me + 1).start()
-
-    @pl.when(me == 0)
-    def _():
-        edge[...] = jnp.zeros_like(edge)
-
     offsets, at = [], 0
     for _, share in ROUTES:
         offsets.append((at * half_cols // 16, share * half_cols // 16))
@@ -166,12 +163,16 @@
     def flat(r, dx, dy):
         return (r * 2 + dx) * 2 + dy
 
-    def hop(r, z_at, dx, dy, move):
+    def hop(r, z_at, dx, dy, move, own):
         ref = part(r, z_at, x ^ dx, grp ^ dy, core)
+        source = ref
+        if own:
+            start, size = offsets[r]
+            source = w_ref.at[:, pl.ds(pl.multiple_of((grp ^ dy) * half_cols + start, 128), size)]
         to = {"up": (grp, me + 4), "down": (grp, me - 4), "x": (grp, me ^ 2), "y": (1 - grp, me)}[move]
         there = flat(r, dx ^ 1 if move == "x" else dx, dy ^ 1 if move == "y" else dy)
         return pltpu.make_async_remote_copy(
-            src_ref=ref, dst_ref=ref, send_sem=send_sems.at[slots[(r, dx, dy, move)] * Z_SIZE + z_at],
+            src_ref=source, dst_ref=ref, send_sem=send_sems.at[slots[(r, dx, dy, move)] * Z_SIZE + z_at],
             recv_sem=recv_sems.at[there * Z_SIZE + z_at], device_id=to, device_id_type=MESH_ID)
 
     def share_core(r, z_at, dx, dy, c_at):
@@ -183,7 +184,7 @@
 
     def share_full(c_at):
         return pltpu.make_async_remote_copy(
-            src_ref=own_rows(c_at), dst_ref=own_rows(c_at), send_sem=full_sems.at[0], recv_sem=full_sems.at[1],
+            src_ref=w_ref, dst_ref=own_rows(c_at), send_sem=full_sems.at[0], recv_sem=full_sems.at[1],
             device_id=(grp, me ^ 1), device_id_type=MESH_ID)
 
     def when_valid(dz, action):
@@ -212,7 +213,7 @@
                     src_ref=ref, dst_ref=ref, send_sem=sem, recv_sem=sem,
                     device_id=(grp, me ^ 1), device_id_type=MESH_ID).wait_recv()
             for move in sends_of(ROUTES[r][0], dz, dx, dy):
-                when_move(move, lambda move=move: hop(r, z_at, dx, dy, move).start())
+                when_move(move, lambda move=move: hop(r, z_at, dx, dy, move, dz == 0 and dx == 0).start())
             if dz != 0 or dx != 0:
                 share_core(r, z_at, dx, dy, core).start()
         when_valid(dz, action)
@@ -221,7 +222,6 @@
     if gathers:
         local = pltpu.make_async_copy(w_ref, own_rows(core), local_sem)
         local.start()
-        local.wait()
         for _, dz, dx, dy, r in sites:
             if dz == 0 and dx == 0:
                 visit(dz, dx, dy, r)
@@ -229,6 +229,18 @@
     else:
         local = pltpu.make_async_copy(w_ref, wbuf, local_sem)
         local.start()
+
+    for load in loads[:3]:
+        load.wait()
+
+    @pl.when(me + 1 < seq)
+    def _():
+        for i, ref in enumerate((q_ref, k_ref, v_ref)):
+            edge_copy(i, ref, me + 1).start()
+
+    @pl.when(me == 0)
+    def _():
+        edge[...] = jnp.zeros_like(edge)
 
     def columns(i):
         return pl.ds(pl.multiple_of(i * width, width), width)
@@ -279,7 +291,13 @@
         conv[BLOCK:, cols] = low
         return carry
 
-    lax.fori_loop(0, chan // width, forward_chunk, 0)
+    quarter = chan // width // 4
+    for turn in range(4):
+        lax.fori_loop(turn * quarter, (turn + 1) * quarter, forward_chunk, 0)
+        if gathers and turn > 0:
+            for level, dz, dx, dy, r in sites:
+                if level == 1 and (abs(dz), dx, dy) == ((1, 0, 0), (0, 1, 0), (9, 9, 9))[turn - 1]:
+                    visit(dz, dx, dy, r)
 
     def state_copy(own, into, sems, k, target):
         return pltpu.make_async_remote_copy(
@@ -311,10 +329,6 @@
         return total
 
     send_states(e_own, e_in, e_sems, 1)
-    if gathers:
-        for level, dz, dx, dy, r in sites:
-            if level == 1 and (dz != 0 or dx != 0):
-                visit(dz, dx, dy, r)
     take_states(e_own, e_in, e_sems, 1)
     kept_f = [free(per_dev * (me - k + 1), first) for k in range(1, REACH + 1)]
     kept_b = [free(first + per_dev + 1, first + per_dev * k + 1) for k in range(1, REACH + 1)]
@@ -337,6 +351,7 @@
 
     lax.fori_loop(0, chan // width, forward_finish, 0)
     acc[...] = jnp.zeros_like(acc)
+    loads[3].wait()
 
     tile = 512
 
@@ -364,11 +379,12 @@
             acc[:, at] = acc[:, at] + jnp.dot(gated[:, cols], wbuf[j, :, at], preferred_element_type=F32)
             return carry
 
-        lax.fori_loop(0, acc.shape[1] // tile, mixed, 0)
+        lax.fori_loop(0, acc.shape[1] // tile, mixed, 0, unroll=8)
 
     def settle(dz, dx):
         def action(z_at):
             if dz == 0 and dx == 0:
+                local.wait()
                 share_full(1 - core).wait_recv()
             else:
                 for dy in range(2):
@@ -381,12 +397,16 @@
         top_level = max(site[0] for site in sites)
         pairs = sorted((abs(dz) + dx + 1, dz, dx) for dz in range(1 - Z_SIZE, Z_SIZE) for dx in range(2))
         for level in range(2, top_level + 2):
-            for site_level, dz, dx, dy, r in sites:
-                if site_level == level and (dz != 0 or dx != 0):
-                    visit(dz, dx, dy, r)
-            for pair_level, dz, dx in pairs:
-                if pair_level == level - 1:
-                    settle(dz, dx)
+            ready = [pair[1:] for pair in pairs if pair[0] == level - 1]
+            groups = sorted({site[1:4] for site in sites if site[0] == level and (site[1] != 0 or site[2] != 0)},
+                            key=lambda at: (at[2], at[1], at[0]))
+            for count, at in enumerate(groups):
+                for r in range(len(ROUTES)):
+                    visit(*at, r)
+                if count % 2 == 1 and ready:
+                    settle(*ready.pop(0))
+            for pair in ready:
+                settle(*pair)
         for pair_level, dz, dx in pairs:
             if pair_level > top_level:
                 settle(dz, dx)
@@ -407,6 +427,9 @@
         return carry
 
     lax.fori_loop(0, acc.shape[1] // tile, write_mixed, 0)
+    stores = [pltpu.make_async_copy(a, b, out_sems.at[i]) for i, (a, b) in enumerate(
+        ((out_ref, out_hbm), (gq_ref, gq_hbm), (gk_ref, gk_hbm), (gv_ref, gv_hbm)))]
+    stores[0].start()
     take_states(b_own, b_in, b_sems, -1)
 
     def backward_finish(i, carry):
@@ -465,6 +488,9 @@
 
     lax.fori_loop(0, chan // width, backward_short, 0)
 
+    for store in stores[1:]:
+        store.start()
+
     @pl.when(me + 1 < seq)
     def _():
         for i, ref in enumerate((q_ref, k_ref, v_ref)):
@@ -485,10 +511,33 @@
         for _, dz, dx, dy, r in sites:
             def action(z_at):
                 for move in sends_of(ROUTES[r][0], dz, dx, dy):
-                    when_move(move, lambda move=move: hop(r, z_at, dx, dy, move).wait_send())
+                    when_move(move, lambda move=move: hop(r, z_at, dx, dy, move, dz == 0 and dx == 0).wait_send())
                 if dz != 0 or dx != 0:
                     share_core(r, z_at, dx, dy, core).wait_send()
             when_valid(dz, action)
+
+    for store in stores:
+        store.wait()
+
+
+def hand_on(*refs):
+    count = (len(refs) - 2) // 3
+    sems, back_sems = refs[-2:]
+    takes, gives = [], []
+    for i in range(count):
+        rows = refs[i].shape[0] // 4
+        for t in range(4):
+            at = pl.ds(t * rows, rows)
+            held = refs[2 * count + i].at[at]
+            takes.append(pltpu.make_async_copy(refs[i].at[at], held, sems.at[i * 4 + t]))
+            gives.append(pltpu.make_async_copy(held, refs[count + i].at[at], back_sems.at[i * 4 + t]))
+    for take in takes:
+        take.start()
+    for take, give in zip(takes, gives):
+        take.wait()
+        give.start()
+    for give in gives:
+        give.wait()
 
 
 def on_device(queries, key_inputs, values, short_taps, decay_rates, residues, skip_gain, out_weight, cotangent,
@@ -504,7 +553,8 @@
     dma = pltpu.SemaphoreType.DMA
     count = len(ROUTES) * 4 * Z_SIZE
     full = (rows, chan)
-    return pl.pallas_call(
+    anywhere = pl.BlockSpec(memory_space=pl.ANY)
+    outs = pl.pallas_call(
         functools.partial(kernel, seq, gathers),
         out_shape=(
             jax.ShapeDtypeStruct((rows, model), BF16),
@@ -512,10 +562,11 @@
             jax.ShapeDtypeStruct(full, BF16),
             jax.ShapeDtypeStruct(full, BF16),
         ),
-        in_specs=[pl.BlockSpec(memory_space=pltpu.SMEM)] + [vmem] * 7
-        + [pl.BlockSpec(memory_space=pl.ANY)] + [vmem],
-        out_specs=(vmem,) * 4,
+        in_specs=[pl.BlockSpec(memory_space=pltpu.SMEM)] + [anywhere] * 3 + [vmem] * 4 + [anywhere] * 2,
+        out_specs=(anywhere,) * 4,
         scratch_shapes=[
+            pltpu.VMEM(full, BF16), pltpu.VMEM(full, BF16), pltpu.VMEM(full, BF16), pltpu.VMEM((rows, model), BF16),
+            pltpu.VMEM((rows, model), BF16), pltpu.VMEM(full, BF16), pltpu.VMEM(full, BF16), pltpu.VMEM(full, BF16),
             pltpu.VMEM((pairs, 256, model), BF16),
             pltpu.VMEM(full, F32), pltpu.VMEM(full, F32), pltpu.VMEM(full, F32), pltpu.VMEM(full, F32),
             pltpu.VMEM(full, BF16),
@@ -526,12 +577,20 @@
             pltpu.VMEM((2, chan), F32), pltpu.VMEM((REACH, 2, chan), F32),
             pltpu.VMEM((2, chan), F32), pltpu.VMEM((REACH, 2, chan), F32),
             dma((6,)), dma((2,)), dma((2, REACH)), dma((2, REACH)), dma,
-            dma((count,)), dma((len(send_slots()) * Z_SIZE,)), dma((2, count)), dma((2,)),
+            dma((count,)), dma((len(send_slots()) * Z_SIZE,)), dma((2, count)), dma((2,)), dma((4,)), dma((4,)),
         ],
         compiler_params=pltpu.CompilerParams(
             collective_id=0, has_side_effects=True, vmem_limit_bytes=60 * 1024 * 1024),
     )(doc_blocks, queries, key_inputs, values, short_taps, decay_rates, residues, skip_gain.reshape(1, chan),
       out_weight, cotangent)
+    return pl.pallas_call(
+        hand_on,
+        out_shape=tuple(jax.ShapeDtypeStruct(o.shape, o.dtype) for o in outs),
+        in_specs=[anywhere] * 4,
+        out_specs=(anywhere,) * 4,
+        scratch_shapes=[pltpu.VMEM(o.shape, o.dtype) for o in outs] + [dma((16,)), dma((16,))],
+        compiler_params=pltpu.CompilerParams(vmem_limit_bytes=32 * 1024 * 1024),
+    )(*outs)
 
 
 def solution(mesh):

time: 112 us -> 108 us (0.964); the launches traced: 110 us -> 107 us
  Pallas kernels: 103 us -> 101 us
    pallas_call x1, Pallas kernels: 103 us -> 98.2 us  [on_device(): pl.pallas_call(functools.partial(kernel, seq, gathers), out_shape=(jax.Sh...]
    pallas_call x0 -> x1, Pallas kernels: none -> 2.96 us  [on_device(): pl.pallas_call(hand_on, out_shape=tuple((jax.ShapeDtypeStruct(o.shape, o....]
    unnamed x10 -> x8, local copies, waits for them, and re-layouts: 6.2 us -> 5.26 us
where the time goes in v2:
time: 108 us; the launch traced here: 107 us
  Pallas kernels  101 us (94%)
  local copies, waits for them, and re-layouts  5.26 us (5%)
    pallas_call x1, Pallas kernels, on_device(): pl.pallas_call(functools.partial(kernel, seq, gathers), out_shape=(jax.Sh...  98.2 us
    unnamed x8, local copies, waits for them, and re-layouts  5.26 us
    pallas_call x1, Pallas kernels, on_device(): pl.pallas_call(hand_on, out_shape=tuple((jax.ShapeDtypeStruct(o.shape, o....  2.96 us

profile of v2, /device:TPU:3, one launch (start us, length us, event | category | flops | bytes accessed | tf_op | source)
XLA Modules:
  0.0 107.3 jit_solution(2683344351113486102)
XLA Ops:
  0.6 98.2 %shard_map.129 = (bf16[256,4096]{1,0:T(8,128)(2,1)}, bf16[256,2048]{1,0:T(8,128)(2,1)}, bf16[256,2048]{1,0:T(8,128)(2,1)}, bf16[256,2048]{1,0:T(8,128)(2,1)}) custom-call(s32[4]{0:T(128)} %docs_ref.1, bf16[256,2048]{1,0:T(8,128)(2,1)} %q_hbm.1, bf16[256,2048]{1,0:T(8,128)(2,1)} %k_hbm.1, bf16[256,2048]{1,0:T(8,128)(2,1)} %v_hbm.1, f32[3,3,2048]{2,1,0:T(4,128)} %taps_ref.1, ...), custom_call_target="tpu_custom_call" | custom-call | tf_op jit(solution)/shard_map/pallas_call | solution.py:557
  98.9 0.0 copy-start
  98.9 1.6 %copy-done = bf16[256,4096]{1,0:T(8,128)(2,1)S(1)} copy-done((bf16[256,4096]{1,0:T(8,128)(2,1)S(1)}, bf16[256,4096]{1,0:T(8,128)(2,1)}, u32[]{:S(2)}) %copy-start) | copy-done | bytes 2097176
  100.5 0.0 copy-start.1
  100.5 1.2 %copy-done.1 = bf16[256,2048]{1,0:T(8,128)(2,1)S(1)} copy-done((bf16[256,2048]{1,0:T(8,128)(2,1)S(1)}, bf16[256,2048]{1,0:T(8,128)(2,1)}, u32[]{:S(2)}) %copy-start.1) | copy-done | bytes 1048600
  101.7 0.0 copy-start.2
  101.7 1.2 %copy-done.2 = bf16[256,2048]{1,0:T(8,128)(2,1)S(1)} copy-done((bf16[256,2048]{1,0:T(8,128)(2,1)S(1)}, bf16[256,2048]{1,0:T(8,128)(2,1)}, u32[]{:S(2)}) %copy-start.2) | copy-done | bytes 1048600
  102.9 0.0 copy-start.3
  102.9 1.2 %copy-done.3 = bf16[256,2048]{1,0:T(8,128)(2,1)S(1)} copy-done((bf16[256,2048]{1,0:T(8,128)(2,1)S(1)}, bf16[256,2048]{1,0:T(8,128)(2,1)}, u32[]{:S(2)}) %copy-start.3) | copy-done | bytes 1048600
  104.1 3.0 %shard_map.130 = (bf16[256,4096]{1,0:T(8,128)(2,1)}, bf16[256,2048]{1,0:T(8,128)(2,1)}, bf16[256,2048]{1,0:T(8,128)(2,1)}, bf16[256,2048]{1,0:T(8,128)(2,1)}) custom-call(bf16[256,4096]{1,0:T(8,128)(2,1)S(1)} %copy-done, bf16[256,2048]{1,0:T(8,128)(2,1)S(1)} %copy-done.1, bf16[256,2048]{1,0:T(8,128)(2,1)S(1)} %copy-done.2, bf16[256,2048]{1,0:T(8,128)(2,1)S(1)} %copy-done.3), custom_call_target="tpu_custom_call" | custom-call | tf_op jit(solution)/shard_map/pallas_call | solution.py:586
Async XLA Ops:
  98.9 1.6 %copy-start = (bf16[256,4096]{1,0:T(8,128)(2,1)S(1)}, bf16[256,4096]{1,0:T(8,128)(2,1)}, u32[]{:S(2)}) copy-start(bf16[256,4096]{1,0:T(8,128)(2,1)} %get-tuple-element.8.refs_0_) | copy-start | bytes 6291460
  100.5 1.2 %copy-start.1 = (bf16[256,2048]{1,0:T(8,128)(2,1)S(1)}, bf16[256,2048]{1,0:T(8,128)(2,1)}, u32[]{:S(2)}) copy-start(bf16[256,2048]{1,0:T(8,128)(2,1)} %get-tuple-element.9.refs_1_) | copy-start | bytes 3145732
  101.7 1.2 %copy-start.2 = (bf16[256,2048]{1,0:T(8,128)(2,1)S(1)}, bf16[256,2048]{1,0:T(8,128)(2,1)}, u32[]{:S(2)}) copy-start(bf16[256,2048]{1,0:T(8,128)(2,1)} %get-tuple-element.10.refs_2_) | copy-start | bytes 3145732
  102.9 1.2 %copy-start.3 = (bf16[256,2048]{1,0:T(8,128)(2,1)S(1)}, bf16[256,2048]{1,0:T(8,128)(2,1)}, u32[]{:S(2)}) copy-start(bf16[256,2048]{1,0:T(8,128)(2,1)} %get-tuple-element.11.refs_3_) | copy-start | bytes 3145732
